TPU v7x, 256 devices: a whole 4x4x8 slice. The times are simulated.
256 devices in a mesh: ctx: 64 (over x_hi, y, z), head: 4 (over x_lo, core).
Axes of the slice: x: 4 (x_hi: 2, x_lo: 2; x = x_hi * 2 + x_lo), y: 4, z: 8, core: 2. Of those that a mesh axis runs over, the one named last changes fastest.
Arguments:
- queries: bfloat16 [16384, 6144], P(('ctx', 'head')), may hold values from -42 to 42
- key_head_columns: bfloat16 [16384, 512], P(('ctx', 'head')), may hold values from -4 to 4
- value_head_columns: bfloat16 [16384, 512], P(('ctx', 'head')), may hold values from -6 to 6
- output_gradient: bfloat16 [16384, 6144], P(('ctx', 'head')), may hold values from -6 to 6
- file_starts: int32 [33], replicated, may hold values from 0 to 16320, as said below
- file_imports: int32 [33, 4], replicated, may hold values from -1 to 32, as said below
- header_lens: int32 [33], replicated, may hold values from 16 to 64
Outputs:
- grad_queries: float32 [16384, 6144], P(('ctx', 'head'))
- key_gradient: float32 [16384, 512], P(('ctx', 'head'))
- value_gradient: float32 [16384, 512], P(('ctx', 'head'))
Inputs may be any that keep to these rules, and one draw needn't show every extreme that they name: `file_starts`: Increasing; the first is 0 and the last is 16320; each is a multiple of 64; no two lie in the same aligned block of 256 tokens; each file has 64 tokens or more. `file_imports`: each row lists distinct files other than its own, then -1 in the unused places; file 0 imports nothing.
All inputs are finite; a program needn't handle non-finite values.
Results may differ from a plain program's by a relative error of at most 0.004.
Values may be sent and summed in bfloat16 or wider, within the bound.
A program may use at most 64 MiB of HBM per device.

v0:
```python
import math
import jax
import jax.numpy as jnp
from jax import lax
from jax.sharding import Mesh
from jax.sharding import PartitionSpec as P

WIN = 1024
HDR = 64
HEAD = ("head_0", "head_1")
CTX = ("ctx_0", "ctx_1", "ctx_2")
CTX_HEAD = ("ctx_0", "ctx_1", "ctx_2", "head_0", "head_1")


def in_blocks(array, dim, devices):
    before, after = (array.shape[:dim], array.shape[dim + 1 :])
    return jnp.moveaxis(array.reshape(*before, devices, -1, *after), dim, 0)


def joined_along(parts, dim):
    dims = list(parts.shape[1:])
    dims[dim] *= parts.shape[0]
    return jnp.moveaxis(parts, 0, dim).reshape(dims)


def exchange_in_order(parts, axes, turns):
    dims = [lax.axis_size(a) for a in axes]
    parts = parts.reshape(*dims, *parts.shape[1:])
    for k in turns:
        parts = lax.all_to_all(parts, axes[k], split_axis=k, concat_axis=k, tiled=True)
    return parts.reshape(-1, *parts.shape[len(axes) :])


def two_step_exchange(array, groups, turns, split_dim, concat_dim):
    devices = lax.axis_size(groups[0]) * lax.axis_size(groups[1])
    parts = in_blocks(array, split_dim, devices)
    return joined_along(exchange_in_order(parts, groups, turns), concat_dim)


def passed_along(value, axis, steps):
    count = lax.axis_size(axis)
    first, last = (max(0, -steps), min(count, count - steps))
    return lax.ppermute(value, axis, [(source, source + steps) for source in range(first, last)])


def stacked_from(array, axes, turns):
    parts = array[None]
    for k in turns:
        parts = lax.all_gather(parts, axes[k], axis=0, tiled=True)
    carried = [lax.axis_size(axes[k]) for k in reversed(turns)]
    parts = parts.reshape(*carried, *array.shape)
    turned = sorted(range(len(turns)), key=lambda place: turns[len(turns) - 1 - place])
    return parts.transpose(*turned, *range(len(turns), parts.ndim)).reshape(-1, *array.shape)


def gather_axes(array, axes, turns, dim):
    return joined_along(stacked_from(array, axes, turns), dim)


def own_block(parts, axes, turns):
    inside = parts.shape[1:]
    parts = parts.reshape(*(lax.axis_size(a) for a in axes), *inside)
    parts = jnp.moveaxis(parts, turns, range(len(axes))).reshape(-1, *inside)
    for k in turns:
        parts = lax.psum_scatter(parts, axes[k], scatter_dimension=0, tiled=True)
    return parts[0]


def sum_by_axis(array, axes, turns, dim):
    devices = lax.axis_size(axes)
    return own_block(in_blocks(array, dim, devices), axes, turns)


def local_files(file_starts, file_imports, header_lens, offset_base, span_rows):
    places = offset_base + jnp.arange(span_rows, dtype=jnp.int32)
    before = file_starts[None, :] <= places[:, None]
    file_of = jnp.sum(before.astype(jnp.int32), axis=1) - 1
    file_begin = jnp.max(jnp.where(before, file_starts[None, :], 0), axis=1)
    lower_file = file_of[0]
    upper_file = file_of[span_rows - 1]
    per_file = file_imports.shape[1]
    lower_list = lax.dynamic_slice_in_dim(file_imports, lower_file, 1, 0)[0]
    upper_list = lax.dynamic_slice_in_dim(file_imports, upper_file, 1, 0)[0]
    targets = jnp.concatenate([lower_list, upper_list])
    source_file = jnp.concatenate(
        [jnp.full((per_file,), lower_file, jnp.int32), jnp.full((per_file,), upper_file, jnp.int32)]
    )
    usable = (targets >= 0) & (
        (jnp.arange(2 * per_file, dtype=jnp.int32) < per_file) | (upper_file != lower_file)
    )
    matches = jnp.arange(file_starts.shape[0], dtype=jnp.int32)[None, :] == targets[:, None]
    target_start = jnp.sum(jnp.where(matches, file_starts[None, :], 0), axis=1)
    target_len = jnp.sum(jnp.where(matches, header_lens[None, :], 0), axis=1)
    return (places, file_of, file_begin, source_file, usable, target_start, target_len)


def visibility(places, file_of, file_begin, key_places, source_file, usable, target_len):
    window_ok = (
        (key_places[None, :] <= places[:, None])
        & (key_places[None, :] > places[:, None] - WIN)
        & (key_places[None, :] >= file_begin[:, None])
    )
    offsets = jnp.arange(usable.shape[0] * HDR, dtype=jnp.int32) % HDR
    header_ok = jnp.repeat(usable, HDR) & (offsets < jnp.repeat(target_len, HDR))
    header_vis = header_ok[None, :] & (file_of[:, None] == jnp.repeat(source_file, HDR)[None, :])
    return jnp.concatenate([window_ok, header_vis], axis=1)


def per_device(
    queries,
    key_head_columns,
    value_head_columns,
    output_gradient,
    file_starts,
    file_imports,
    header_lens,
):
    query_rows, key_rows, value_rows, grad_rows = (
        two_step_exchange(queries, ("head_0", "head_1"), (1, 0), 1, 0),
        two_step_exchange(key_head_columns, ("head_0", "head_1"), (1, 0), 1, 0),
        two_step_exchange(value_head_columns, ("head_0", "head_1"), (1, 0), 1, 0),
        two_step_exchange(output_gradient, ("head_0", "head_1"), (1, 0), 1, 0),
    )
    tokens_here = key_rows.shape[0]
    head_size = key_rows.shape[1]
    queries_per_group = query_rows.shape[1] // head_size
    shard_index = lax.axis_index(CTX)
    ctx_count = lax.axis_size(CTX)
    offset_base = shard_index * tokens_here
    scaling = 1.0 / math.sqrt(head_size)
    reach = WIN // tokens_here
    places, file_of, file_begin, source_file, usable, target_start, target_len = local_files(
        file_starts, file_imports, header_lens, offset_base, tokens_here
    )
    block_count = source_file.shape[0]
    stacked = jnp.concatenate([key_rows, value_rows], axis=1)
    earlier = []
    moving = stacked
    for distance in range(1, reach + 1):
        moving = passed_along(moving, CTX, 1)
        earlier.append(moving)
    inside = (file_starts >= offset_base) & (file_starts < offset_base + tokens_here)
    own_offset = jnp.sum(jnp.where(inside, file_starts - offset_base, 0))
    own_header = lax.dynamic_slice_in_dim(stacked, own_offset, HDR, 0)
    all_headers = gather_axes(own_header, CTX, (0, 2, 1), 0)
    header_rows = jnp.concatenate(
        [
            lax.dynamic_slice_in_dim(all_headers, target_start[index] // tokens_here * HDR, HDR, 0)
            for index in range(block_count)
        ],
        axis=0,
    )
    key_table = jnp.concatenate(earlier[::-1] + [stacked, header_rows], axis=0)
    key_matrix = key_table[:, :head_size]
    value_matrix = key_table[:, head_size:]
    window_len = (reach + 1) * tokens_here
    key_places = offset_base - reach * tokens_here + jnp.arange(window_len, dtype=jnp.int32)
    visible = visibility(places, file_of, file_begin, key_places, source_file, usable, target_len)
    heads_block = max(
        (
            divisor
            for divisor in range(1, queries_per_group + 1)
            if queries_per_group % divisor == 0 and divisor * tokens_here <= max(512, tokens_here)
        )
    )
    block_total = queries_per_group // heads_block
    query_blocks = (
        query_rows.reshape(tokens_here, queries_per_group, head_size)
        .transpose(1, 0, 2)
        .reshape(block_total, heads_block, tokens_here, head_size)
    )
    grad_blocks = (
        grad_rows.reshape(tokens_here, queries_per_group, head_size)
        .transpose(1, 0, 2)
        .reshape(block_total, heads_block, tokens_here, head_size)
    )

    def attend(carry, inputs):
        key_gradient_sum, value_gradient_sum = carry
        query_block, grad_block = inputs
        scores = (
            jnp.einsum("htd,kd->htk", query_block, key_matrix, preferred_element_type=jnp.float32)
            * scaling
        )
        scores = jnp.where(visible[None], scores, -jnp.inf)
        ceiling = jnp.max(scores, axis=-1, keepdims=True)
        log_total = ceiling + jnp.log(jnp.sum(jnp.exp(scores - ceiling), axis=-1, keepdims=True))
        weights = jnp.exp(scores - log_total)
        grad_weights = jnp.einsum(
            "htd,kd->htk", grad_block, value_matrix, preferred_element_type=jnp.float32
        )
        centre = jnp.sum(weights * grad_weights, axis=-1, keepdims=True)
        grad_scores = (weights * (grad_weights - centre)).astype(jnp.bfloat16)
        weights_low = weights.astype(jnp.bfloat16)
        grad_query = (
            jnp.einsum("htk,kd->htd", grad_scores, key_matrix, preferred_element_type=jnp.float32)
            * scaling
        )
        key_gradient_sum = (
            key_gradient_sum
            + jnp.einsum(
                "htk,htd->kd", grad_scores, query_block, preferred_element_type=jnp.float32
            )
            * scaling
        )
        value_gradient_sum = value_gradient_sum + jnp.einsum(
            "htk,htd->kd", weights_low, grad_block, preferred_element_type=jnp.float32
        )
        return ((key_gradient_sum, value_gradient_sum), grad_query)

    empty_gradient = jnp.zeros((key_table.shape[0], head_size), jnp.float32)
    (key_gradient_sum, value_gradient_sum), grad_query = lax.scan(
        attend, (empty_gradient, empty_gradient), (query_blocks, grad_blocks)
    )
    grad_query = (
        grad_query.reshape(queries_per_group, tokens_here, head_size)
        .transpose(1, 0, 2)
        .reshape(tokens_here, queries_per_group * head_size)
    )
    combined = jnp.concatenate([key_gradient_sum, value_gradient_sum], axis=1)

    def window_part(index):
        return combined[index * tokens_here : (index + 1) * tokens_here]

    collected = window_part(reach)
    carried = window_part(0)
    for distance in range(1, reach + 1):
        carried = passed_along(carried, CTX, -1)
        if distance < reach:
            carried = carried + window_part(distance)
    collected = collected + carried
    header_part = combined[window_len:]
    slot_table = jnp.zeros((ctx_count * HDR, 2 * head_size), jnp.float32)
    for index in range(block_count):
        at_row = target_start[index] // tokens_here * HDR
        current = lax.dynamic_slice_in_dim(slot_table, at_row, HDR, 0)
        slot_table = lax.dynamic_update_slice_in_dim(
            slot_table, current + header_part[index * HDR : (index + 1) * HDR], at_row, 0
        )
    arriving = sum_by_axis(slot_table, CTX, (1, 2, 0), 0)
    current = lax.dynamic_slice_in_dim(collected, own_offset, HDR, 0)
    collected = lax.dynamic_update_slice_in_dim(collected, current + arriving, own_offset, 0)
    grad_queries, key_gradient, value_gradient = (
        lax.all_to_all(grad_query, HEAD, split_axis=0, concat_axis=1, tiled=True),
        lax.all_to_all(collected[:, :head_size], HEAD, split_axis=0, concat_axis=1, tiled=True),
        lax.all_to_all(collected[:, head_size:], HEAD, split_axis=0, concat_axis=1, tiled=True),
    )
    return (grad_queries, key_gradient, value_gradient)


def solution(mesh):
    split = Mesh(
        mesh.devices.reshape(2, 4, 8, 2, 2), ("ctx_0", "ctx_1", "ctx_2", "head_0", "head_1")
    )
    placed = (
        P(CTX_HEAD, None),
        P(CTX_HEAD, None),
        P(CTX_HEAD, None),
        P(CTX_HEAD, None),
        P(),
        P(),
        P(),
    )
    return jax.shard_map(
        per_device,
        mesh=split,
        in_specs=placed,
        out_specs=(P(CTX_HEAD, None), P(CTX_HEAD, None), P(CTX_HEAD, None)),
        check_vma=False,
    )
```

profile of v0, /device:TPU:1, one launch (start us, length us, event | category | flops | bytes accessed | tf_op | source)
XLA Modules:
  0.0 381.8 jit_solution(10581533873204575703)
XLA Ops:
  8.7 6.5 %all-to-all-start.4 = ((bf16[2,2,64,128]{3,2,0,1:T(8,128)(2,1)}), bf16[2,2,64,128]{3,2,0,1:T(8,128)(2,1)S(1)}, u32[]{:S(2)}, u32[]{:S(2)}) async-start(bf16[2,2,64,128]{3,2,0,1:T(8,128)(2,1)} %copy.125), calls=%async_computation.4 | async-start | bytes 131072 | tf_op jit(solution)/shard_map/all_to_all | solution.py:30
  16.7 3.3 all-to-all-start.2
  21.1 3.3 all-to-all-start.5
  27.3 3.3 all-to-all-start.3
  34.0 4.9 %all-gather = bf16[128,256]{1,0:T(8,128)(2,1)S(1)} all-gather(bf16[64,256]{1,0:T(8,128)(2,1)S(1)} %fusion.33), channel_id=2, replica_groups=mesh['ctx_0'=2,'ctx_1'=4,'ctx_2'=8,'head_0'=2,'head_1'=2] {'ctx_0'}, dimensions={0}, use_global_device_ids=true | all-gather | bytes 98304 | tf_op jit(solution)/shard_map/all_gather | solution.py:49
  38.9 23.3 %all_gather.10 = bf16[16,64,256]{2,1,0:T(8,128)(2,1)} all-gather(bf16[2,64,256]{2,1,0:T(8,128)(2,1)S(1)} %bitcast.156), channel_id=1, replica_groups=mesh['ctx_0'=2,'ctx_1'=4,'ctx_2'=8,'head_0'=2,'head_1'=2] {'ctx_2'}, dimensions={0}, use_global_device_ids=true | all-gather | bytes 589824 | tf_op jit(solution)/shard_map/all_gather | solution.py:49
  65.6 13.0 %all-to-all-start.6 = ((bf16[2,2,64,1536]{3,2,0,1:T(8,128)(2,1)}), bf16[2,2,64,1536]{3,2,0,1:T(8,128)(2,1)S(1)}, u32[]{:S(2)}, u32[]{:S(2)}) async-start(bf16[2,2,64,1536]{3,2,0,1:T(8,128)(2,1)} %copy.129), calls=%async_computation.6 | async-start | bytes 1572864 | tf_op jit(solution)/shard_map/all_to_all | solution.py:30
  86.2 3.6 all-to-all-start
  91.5 2.6 collective-permute-start
  94.2 3.6 all-to-all-start.7
  121.9 2.6 collective-permute-start.1
  127.1 4.1 %collective-permute-start.2 = (bf16[256,256]{1,0:T(8,128)(2,1)S(1)}, bf16[256,256]{1,0:T(8,128)(2,1)S(1)}, u32[]{:S(2)}, u32[]{:S(2)}) collective-permute-start(bf16[256,256]{1,0:T(8,128)(2,1)S(1)} %collective-permute-done.1), channel_id=1, source_target_pairs={{0,4},{4,8},{8,12},{12,16},{16,20},{20,24},{24,28},{28,32},{32,36}... | collective-permute-start | bytes 393224 | tf_op jit(solution)/shard_map/ppermute | solution.py:43
  131.2 4.3 %all-to-all-start.1 = ((bf16[2,2,64,1536]{3,2,1,0:T(8,128)(2,1)}), bf16[2,2,64,1536]{3,2,1,0:T(8,128)(2,1)}, u32[]{:S(2)}, u32[]{:S(2)}) async-start(bf16[2,2,64,1536]{3,2,1,0:T(8,128)(2,1)} %copy.119), calls=%async_computation.1 | async-start | bytes 1572864 | tf_op jit(solution)/shard_map/all_to_all | solution.py:30
  135.8 2.8 collective-permute-start.3
  141.6 3.5 all-to-all-done.1
  160.9 67.9 %while.15 = (s32[]{:T(128)}, f32[1792,128]{1,0:T(8,128)S(1)}, f32[1792,128]{1,0:T(8,128)}, f32[6,2,256,128]{3,2,1,0:T(8,128)}, pred[256,1792]{1,0:T(8,128)(4,1)S...) while((s32[]{:T(128)}, f32[1792,128]{1,0:T(8,128)S(1)}, ...), condition=%wide.region_9.10_spmd.clone, body=%wide.region_5.9_spmd.clone.sunk | while | flops 1188461568 | bytes 80503144 | solution.py:212
  169.0 2.9 fusion.69
  180.1 3.3 fusion.69
  191.5 3.3 fusion.69
  202.8 3.3 fusion.69
  214.2 3.3 fusion.69
  225.6 3.3 fusion.69
  233.0 56.0 %reduce-scatter.4.cloned.1.call-done = f32[16,64,256]{2,1,0:T(8,128)} async-done(((f32[64,64,256]{2,1,0:T(8,128)}), f32[16,64,256]{2,1,0:T(8,128)}) %reduce-scatter.4.cloned.1.call-update) | async-done | bytes 1048592 | tf_op jit(solution)/shard_map/reduce_scatter | solution.py:65
  290.4 7.8 %collective-permute-done.4 = f32[256,256]{1,0:T(8,128)S(1)} collective-permute-done((f32[256,256]{1,0:T(8,128)S(1)}, f32[256,256]{1,0:T(8,128)S(1)}, u32[]{:S(2)}, u32[]{:S(2)}) %collective-permute-start.4) | collective-permute-done | bytes 262176 | tf_op jit(solution)/shard_map/ppermute | solution.py:43
  299.6 8.4 %collective-permute-done.5 = f32[256,256]{1,0:T(8,128)S(1)} collective-permute-done((f32[256,256]{1,0:T(8,128)S(1)}, f32[256,256]{1,0:T(8,128)S(1)}, u32[]{:S(2)}, u32[]{:S(2)}) %collective-permute-start.5) | collective-permute-done | bytes 262176 | tf_op jit(solution)/shard_map/ppermute | solution.py:43
  313.1 7.4 %all-to-all-start.8 = ((f32[4,64,1536]{2,1,0:T(8,128)}), f32[4,64,1536]{2,1,0:T(8,128)S(1)}, u32[]{:S(2)}, u32[]{:S(2)}) async-start(f32[4,64,1536]{2,1,0:T(8,128)} %all_to_all.74), calls=%async_computation.8 | async-start | bytes 3145728 | tf_op jit(solution)/shard_map/all_to_all | solution.py:244
  322.8 4.6 %reduce-scatter.6.cloned.1.call-done = f32[2,64,256]{2,1,0:T(8,128)} async-done(((f32[16,64,256]{2,1,0:T(8,128)}), f32[2,64,256]{2,1,0:T(8,128)}) %reduce-scatter.6.cloned.1.call-update) | async-done | bytes 131088 | tf_op jit(solution)/shard_map/reduce_scatter | solution.py:65
  327.4 4.0 %collective-permute-done.7 = f32[256,256]{1,0:T(8,128)S(1)} collective-permute-done((f32[256,256]{1,0:T(8,128)S(1)}, f32[256,256]{1,0:T(8,128)S(1)}, u32[]{:S(2)}, u32[]{:S(2)}) %collective-permute-start.7) | collective-permute-done | bytes 262176 | tf_op jit(solution)/shard_map/ppermute | solution.py:43
  332.4 24.7 %reduce-scatter.8.cloned.1.call-done = f32[1,64,256]{2,1,0:T(8,128)} async-done(((f32[2,64,256]{2,1,0:T(8,128)}), f32[1,64,256]{2,1,0:T(8,128)}) %reduce-scatter.8.cloned.1.call-update) | async-done | bytes 65552 | tf_op jit(solution)/shard_map/reduce_scatter | solution.py:65
  359.3 3.8 all-to-all-start.10
  366.6 4.3 %all-to-all-start.9 = ((f32[4,64,128]{2,1,0:T(8,128)}), f32[4,64,128]{2,1,0:T(8,128)S(1)}, u32[]{:S(2)}, u32[]{:S(2)}) async-start(f32[4,64,128]{2,1,0:T(8,128)} %bitcast.35), calls=%async_computation.12 | async-start | bytes 262144 | tf_op jit(solution)/shard_map/all_to_all | solution.py:245
  371.6 2.9 all-to-all-done.9
  (260 shorter events, 111.2 us)
Async XLA Ops:
  8.7 8.0 %all-to-all-start.4 = ((bf16[2,2,64,128]{3,2,0,1:T(8,128)(2,1)}), bf16[2,2,64,128]{3,2,0,1:T(8,128)(2,1)S(1)}, u32[]{:S(2)}, u32[]{:S(2)}) async-start(bf16[2,2,64,128]{3,2,0,1:T(8,128)(2,1)} %copy.125), calls=%async_computation.4 | async-start | bytes 131072 | tf_op jit(solution)/shard_map/all_to_all | solution.py:30
  16.7 4.4 %all-to-all-start.2 = ((bf16[2,2,64,128]{3,2,0,1:T(8,128)(2,1)}), bf16[2,2,64,128]{3,2,0,1:T(8,128)(2,1)S(1)}, u32[]{:S(2)}, u32[]{:S(2)}) async-start(bf16[2,2,64,128]{3,2,0,1:T(8,128)(2,1)} %copy.122), calls=%async_computation.2 | async-start | bytes 131072 | tf_op jit(solution)/shard_map/all_to_all | solution.py:30
  21.1 6.3 %all-to-all-start.5 = ((bf16[2,2,64,128]{3,2,1,0:T(8,128)(2,1)}), bf16[2,2,64,128]{3,2,1,0:T(8,128)(2,1)S(1)}, u32[]{:S(2)}, u32[]{:S(2)}) async-start(bf16[2,2,64,128]{3,2,1,0:T(8,128)(2,1)} %copy.126), calls=%async_computation.5 | async-start | bytes 131072 | tf_op jit(solution)/shard_map/all_to_all | solution.py:30
  27.3 6.6 %all-to-all-start.3 = ((bf16[2,2,64,128]{3,2,1,0:T(8,128)(2,1)}), bf16[2,2,64,128]{3,2,1,0:T(8,128)(2,1)S(1)}, u32[]{:S(2)}, u32[]{:S(2)}) async-start(bf16[2,2,64,128]{3,2,1,0:T(8,128)(2,1)} %copy.123), calls=%async_computation.3 | async-start | bytes 131072 | tf_op jit(solution)/shard_map/all_to_all | solution.py:30
  30.6 122.4 %all-gather.3.cloned.1.call-start = ((), (), s32[]{:S(2)}) async-start(), calls=%async_computation.14 | async-start | bytes 2621440 | tf_op jit(solution)/shard_map/all_gather | solution.py:49
  38.9 39.8 %copy-start.11 = (s32[33]{0:T(128)S(1)}, s32[33]{0:T(128)}, u32[]{:S(2)}) copy-start(s32[33]{0:T(128)} %param.13) | copy-start | bytes 400
  38.9 44.3 %copy-start.9 = (bf16[64,6144]{1,0:T(8,128)(2,1)S(1)}, bf16[64,6144]{1,0:T(8,128)(2,1)}, u32[]{:S(2)}) copy-start(bf16[64,6144]{1,0:T(8,128)(2,1)} %param.9) | copy-start | bytes 2359300
  65.6 20.6 %all-to-all-start.6 = ((bf16[2,2,64,1536]{3,2,0,1:T(8,128)(2,1)}), bf16[2,2,64,1536]{3,2,0,1:T(8,128)(2,1)S(1)}, u32[]{:S(2)}, u32[]{:S(2)}) async-start(bf16[2,2,64,1536]{3,2,0,1:T(8,128)(2,1)} %copy.129), calls=%async_computation.6 | async-start | bytes 1572864 | tf_op jit(solution)/shard_map/all_to_all | solution.py:30
  83.2 7.5 %copy-start.10 = (s32[33,4]{0,1:T(4,128)S(1)}, s32[33,4]{0,1:T(4,128)}, u32[]{:S(2)}) copy-start(s32[33,4]{0,1:T(4,128)} %param.14) | copy-start | bytes 1588
  83.9 13.8 %copy-start.12 = (s32[33]{0:T(128)S(1)}, s32[33]{0:T(128)}, u32[]{:S(2)}) copy-start(s32[33]{0:T(128)} %param.15) | copy-start | bytes 400
  86.2 8.0 %all-to-all-start = ((bf16[2,2,64,1536]{3,2,0,1:T(8,128)(2,1)}), bf16[2,2,64,1536]{3,2,0,1:T(8,128)(2,1)S(1)}, u32[]{:S(2)}, u32[]{:S(2)}) async-start(bf16[2,2,64,1536]{3,2,0,1:T(8,128)(2,1)} %copy.118), calls=%async_computation | async-start | bytes 1572864 | tf_op jit(solution)/shard_map/all_to_all | solution.py:30
  91.5 30.4 %collective-permute-start = (bf16[256,256]{1,0:T(8,128)(2,1)S(1)}, bf16[256,256]{1,0:T(8,128)(2,1)S(1)}, u32[]{:S(2)}, u32[]{:S(2)}) collective-permute-start(bf16[256,256]{1,0:T(8,128)(2,1)S(1)} %pad_maximum_fusion), channel_id=1, source_target_pairs={{0,4},{4,8},{8,12},{12,16},{16,20},{20,24},{24,28},{28,32},{32,36}... | collective-permute-start | bytes 393224 | tf_op jit(solution)/shard_map/ppermute | solution.py:43
  94.2 37.1 %all-to-all-start.7 = ((bf16[2,2,64,1536]{3,2,1,0:T(8,128)(2,1)}), bf16[2,2,64,1536]{3,2,1,0:T(8,128)(2,1)S(1)}, u32[]{:S(2)}, u32[]{:S(2)}) async-start(bf16[2,2,64,1536]{3,2,1,0:T(8,128)(2,1)} %copy.130), calls=%async_computation.7 | async-start | bytes 1572864 | tf_op jit(solution)/shard_map/all_to_all | solution.py:30
  121.9 5.2 %collective-permute-start.1 = (bf16[256,256]{1,0:T(8,128)(2,1)S(1)}, bf16[256,256]{1,0:T(8,128)(2,1)S(1)}, u32[]{:S(2)}, u32[]{:S(2)}) collective-permute-start(bf16[256,256]{1,0:T(8,128)(2,1)S(1)} %collective-permute-done), channel_id=1, source_target_pairs={{0,4},{4,8},{8,12},{12,16},{16,20},{20,24},{24,28},{28,32},{32,36}... | collective-permute-start | bytes 393224 | tf_op jit(solution)/shard_map/ppermute | solution.py:43
  127.1 8.7 %collective-permute-start.2 = (bf16[256,256]{1,0:T(8,128)(2,1)S(1)}, bf16[256,256]{1,0:T(8,128)(2,1)S(1)}, u32[]{:S(2)}, u32[]{:S(2)}) collective-permute-start(bf16[256,256]{1,0:T(8,128)(2,1)S(1)} %collective-permute-done.1), channel_id=1, source_target_pairs={{0,4},{4,8},{8,12},{12,16},{16,20},{20,24},{24,28},{28,32},{32,36}... | collective-permute-start | bytes 393224 | tf_op jit(solution)/shard_map/ppermute | solution.py:43
  131.2 13.8 %all-to-all-start.1 = ((bf16[2,2,64,1536]{3,2,1,0:T(8,128)(2,1)}), bf16[2,2,64,1536]{3,2,1,0:T(8,128)(2,1)}, u32[]{:S(2)}, u32[]{:S(2)}) async-start(bf16[2,2,64,1536]{3,2,1,0:T(8,128)(2,1)} %copy.119), calls=%async_computation.1 | async-start | bytes 1572864 | tf_op jit(solution)/shard_map/all_to_all | solution.py:30
  135.5 153.5 %reduce-scatter.4.cloned.1.call-start = ((), (), s32[]{:S(2)}) async-start(), calls=%async_computation.15 | async-start | bytes 5242880 | tf_op jit(solution)/shard_map/reduce_scatter | solution.py:65
  135.8 14.0 %collective-permute-start.3 = (bf16[256,256]{1,0:T(8,128)(2,1)S(1)}, bf16[256,256]{1,0:T(8,128)(2,1)S(1)}, u32[]{:S(2)}, u32[]{:S(2)}) collective-permute-start(bf16[256,256]{1,0:T(8,128)(2,1)S(1)} %collective-permute-done.2), channel_id=1, source_target_pairs={{0,4},{4,8},{8,12},{12,16},{16,20},{20,24},{24,28},{28,32},{32,36}... | collective-permute-start | bytes 393224 | tf_op jit(solution)/shard_map/ppermute | solution.py:43
  183.4 3.6 copy-start.6
  194.8 3.6 copy-start.6
  206.1 3.6 copy-start.6
  217.5 3.6 copy-start.6
  230.2 77.8 %copy-start.8 = (f32[1792,256]{1,0:T(8,128)}, f32[1792,256]{1,0:T(8,128)S(1)}, u32[]{:S(2)}) copy-start(f32[1792,256]{1,0:T(8,128)S(1)} %constant_dynamic-update-slice_fusion.13) | copy-start | bytes 5505028
  233.0 94.4 %reduce-scatter.6.cloned.1.call-start = ((), (), s32[]{:S(2)}) async-start(), calls=%async_computation.16 | async-start | bytes 1179648 | tf_op jit(solution)/shard_map/reduce_scatter | solution.py:65
  289.1 9.1 %collective-permute-start.4 = (f32[256,256]{1,0:T(8,128)S(1)}, f32[256,256]{1,0:T(8,128)S(1)}, u32[]{:S(2)}, u32[]{:S(2)}) collective-permute-start(f32[256,256]{1,0:T(8,128)S(1)} %slice.128), channel_id=1, source_target_pairs={{4,0},{8,4},{12,8},{16,12},{20,16},{24,20},{28,24},{32,28},{36,32}... | collective-permute-start | bytes 786440 | tf_op jit(solution)/shard_map/ppermute | solution.py:43
  298.3 9.7 %collective-permute-start.5 = (f32[256,256]{1,0:T(8,128)S(1)}, f32[256,256]{1,0:T(8,128)S(1)}, u32[]{:S(2)}, u32[]{:S(2)}) collective-permute-start(f32[256,256]{1,0:T(8,128)S(1)} %slice_add_fusion.2), channel_id=1, source_target_pairs={{4,0},{8,4},{12,8},{16,12},{20,16},{24,20},{28,24},{32,28},{36,32}... | collective-permute-start | bytes 786440 | tf_op jit(solution)/shard_map/ppermute | solution.py:43
  308.0 12.5 %collective-permute-start.6 = (f32[256,256]{1,0:T(8,128)S(1)}, f32[256,256]{1,0:T(8,128)S(1)}, u32[]{:S(2)}, u32[]{:S(2)}) collective-permute-start(f32[256,256]{1,0:T(8,128)S(1)} %slice_add_fusion.1), channel_id=1, source_target_pairs={{4,0},{8,4},{12,8},{16,12},{20,16},{24,20},{28,24},{32,28},{36,32}... | collective-permute-start | bytes 786440 | tf_op jit(solution)/shard_map/ppermute | solution.py:43
  313.1 46.2 %all-to-all-start.8 = ((f32[4,64,1536]{2,1,0:T(8,128)}), f32[4,64,1536]{2,1,0:T(8,128)S(1)}, u32[]{:S(2)}, u32[]{:S(2)}) async-start(f32[4,64,1536]{2,1,0:T(8,128)} %all_to_all.74), calls=%async_computation.8 | async-start | bytes 3145728 | tf_op jit(solution)/shard_map/all_to_all | solution.py:244
  320.5 36.6 %reduce-scatter.8.cloned.1.call-start = ((), (), s32[]{:S(2)}) async-start(), calls=%async_computation.17 | async-start | bytes 196608 | tf_op jit(solution)/shard_map/reduce_scatter | solution.py:65
  321.5 9.9 %collective-permute-start.7 = (f32[256,256]{1,0:T(8,128)S(1)}, f32[256,256]{1,0:T(8,128)S(1)}, u32[]{:S(2)}, u32[]{:S(2)}) collective-permute-start(f32[256,256]{1,0:T(8,128)S(1)} %slice_add_fusion), channel_id=1, source_target_pairs={{4,0},{8,4},{12,8},{16,12},{20,16},{24,20},{28,24},{32,28},{36,32}... | collective-permute-start | bytes 786440 | tf_op jit(solution)/shard_map/ppermute | solution.py:43
  359.3 7.4 %all-to-all-start.10 = ((f32[4,64,128]{2,1,0:T(8,128)}), f32[4,64,128]{2,1,0:T(8,128)S(1)}, u32[]{:S(2)}, u32[]{:S(2)}) async-start(f32[4,64,128]{2,1,0:T(8,128)} %bitcast.37), calls=%async_computation.13 | async-start | bytes 262144 | tf_op jit(solution)/shard_map/all_to_all | solution.py:246
  366.6 7.9 %all-to-all-start.9 = ((f32[4,64,128]{2,1,0:T(8,128)}), f32[4,64,128]{2,1,0:T(8,128)S(1)}, u32[]{:S(2)}, u32[]{:S(2)}) async-start(f32[4,64,128]{2,1,0:T(8,128)} %bitcast.35), calls=%async_computation.12 | async-start | bytes 262144 | tf_op jit(solution)/shard_map/all_to_all | solution.py:245
  (44 other events, 121.0 us)
Sparse Core Ops, SparseCore 0:
  62.3 41.5 all-gather.2
  233.1 55.9 reduce-scatter.3
  291.8 35.5 reduce-scatter.5
  329.8 27.2 reduce-scatter.7
where the time goes:
time: 384 us; the launch traced here: 382 us
  waiting for transfers between devices  120 us (31%)
  starting transfers between devices  73.9 us (19%)
  matrix products  57.4 us (15%)
  local copies, waits for them, and re-layouts  45.2 us (12%)
  between operations  41.9 us (11%)
  blocking collectives  28.2 us (7%)
  other arithmetic  14.8 us (4%)
    reduce_scatter x3, waiting for transfers between devices, own_block(): parts = lax.psum_scatter(parts, axes[k], scatter_dimension=0, tiled=True)  85.3 us
    all_to_all x8, starting transfers between devices, exchange_in_order(): lax.all_to_all(parts, axes[k], split_axis=k, concat_axis=k, tiled=True)  40.9 us
    all_gather x2, blocking collectives, stacked_from(): parts = lax.all_gather(parts, axes[k], axis=0, tiled=True)  28.2 us
    ppermute x8, waiting for transfers between devices, passed_along(): lax.ppermute(value, axis, [(source, source + steps) for source in range(f...  22.9 us
    dot_general x6, matrix products, attend(): jnp.einsum('htk,htd->kd', weights_low, grad_block, preferred_element_type...  19.2 us
    ppermute x8, starting transfers between devices, passed_along(): lax.ppermute(value, axis, [(source, source + steps) for source in range(f...  17.3 us
    dot_general x6, matrix products, attend(): jnp.einsum('htk,htd->kd', grad_scores, query_block, preferred_element_typ...  12.5 us
    dot_general x6, matrix products, attend(): jnp.einsum('htd,kd->htk', query_block, key_matrix, preferred_element_type...  11.9 us
  transfers between devices with their start and end apart: 23, of which 12 were waited for; matrix products, arithmetic and copies ran while one was open for 9% of the time, Pallas kernels for 0%

commit v1 on v0

--- a/solution.py
+++ b/solution.py
@@ -46,7 +46,10 @@
 def stacked_from(array, axes, turns):
     parts = array[None]
     for k in turns:
-        parts = lax.all_gather(parts, axes[k], axis=0, tiled=True)
+        devices_2 = lax.axis_size(axes[k])
+        pieces = jnp.stack([parts for _ in range(devices_2)])
+        pieces = lax.all_to_all(pieces, axes[k], split_axis=0, concat_axis=0)
+        parts = jnp.concatenate(pieces, axis=0)
     carried = [lax.axis_size(axes[k]) for k in reversed(turns)]
     parts = parts.reshape(*carried, *array.shape)
     turned = sorted(range(len(turns)), key=lambda place: turns[len(turns) - 1 - place])

time: 384 us -> 399 us (1.039)
  waiting for transfers between devices: 120 us -> 154 us
  blocking collectives: 28.2 us -> 4.35 us
    all_gather x2 -> x0, blocking collectives: 28.2 us -> none  [stacked_from(): parts = lax.all_gather(parts, axes[k], axis=0, tiled=True)]
    all_to_all x8 -> x7, waiting for transfers between devices: 6.21 us -> 21 us  [exchange_in_order(): lax.all_to_all(parts, axes[k], split_axis=k, concat_axis=k, tiled=True)]
    all_to_all x0 -> x3, starting transfers between devices: none -> 13.6 us  [stacked_from(): pieces = lax.all_to_all(pieces, axes[k], split_axis=0, concat_axis=0)]
    all_to_all x8 -> x7, starting transfers between devices: 40.9 us -> 28.5 us  [exchange_in_order(): lax.all_to_all(parts, axes[k], split_axis=k, concat_axis=k, tiled=True)]
    all_to_all x0 -> x3, waiting for transfers between devices: none -> 10.1 us  [stacked_from(): pieces = lax.all_to_all(pieces, axes[k], split_axis=0, concat_axis=0)]
    reduce_scatter x3, waiting for transfers between devices: 85.3 us -> 92.9 us  [own_block(): parts = lax.psum_scatter(parts, axes[k], scatter_dimension=0, tiled=True)]
    all_to_all x0 -> x1, blocking collectives: none -> 4.35 us  [exchange_in_order(): lax.all_to_all(parts, axes[k], split_axis=k, concat_axis=k, tiled=True)]
  transfers between devices with their start and end apart: 23 -> 24, of which waited for: 12 -> 17; matrix products, arithmetic and copies ran while one was open for 9% -> 9% of each run, Pallas kernels for 0% -> 0%
where the time goes in v1:
time: 399 us; the launch traced here: 396 us
  waiting for transfers between devices  154 us (39%)
  starting transfers between devices  75.3 us (19%)
  matrix products  57.5 us (14%)
  local copies, waits for them, and re-layouts  47.4 us (12%)
  between operations  41.3 us (10%)
  other arithmetic  15.4 us (4%)
  blocking collectives  4.35 us (1%)
    reduce_scatter x3, waiting for transfers between devices, own_block(): parts = lax.psum_scatter(parts, axes[k], scatter_dimension=0, tiled=True)  92.9 us
    all_to_all x7, starting transfers between devices, exchange_in_order(): lax.all_to_all(parts, axes[k], split_axis=k, concat_axis=k, tiled=True)  28.5 us
    ppermute x8, waiting for transfers between devices, passed_along(): lax.ppermute(value, axis, [(source, source + steps) for source in range(f...  25 us
    all_to_all x7, waiting for transfers between devices, exchange_in_order(): lax.all_to_all(parts, axes[k], split_axis=k, concat_axis=k, tiled=True)  21 us
    dot_general x6, matrix products, attend(): jnp.einsum('htk,htd->kd', weights_low, grad_block, preferred_element_type...  19.4 us
    ppermute x8, starting transfers between devices, passed_along(): lax.ppermute(value, axis, [(source, source + steps) for source in range(f...  17.6 us
    all_to_all x3, starting transfers between devices, stacked_from(): pieces = lax.all_to_all(pieces, axes[k], split_axis=0, concat_axis=0)  13.6 us
    dot_general x6, matrix products, attend(): jnp.einsum('htk,htd->kd', grad_scores, query_block, preferred_element_typ...  12.5 us
  transfers between devices with their start and end apart: 24, of which 17 were waited for; matrix products, arithmetic and copies ran while one was open for 9% of the time, Pallas kernels for 0%

profile of v1, /device:TPU:1, one launch (start us, length us, event | category | flops | bytes accessed | tf_op | source)
XLA Modules:
  0.0 396.3 jit_solution(12572855513388957938)
XLA Ops:
  8.7 6.5 %all-to-all-start.4 = ((bf16[2,2,64,128]{3,2,0,1:T(8,128)(2,1)}), bf16[2,2,64,128]{3,2,0,1:T(8,128)(2,1)S(1)}, u32[]{:S(2)}, u32[]{:S(2)}) async-start(bf16[2,2,64,128]{3,2,0,1:T(8,128)(2,1)} %copy.125), calls=%async_computation.4 | async-start | bytes 131072 | tf_op jit(solution)/shard_map/all_to_all | solution.py:30
  16.8 3.3 all-to-all-start.2
  21.2 3.3 all-to-all-start.5
  27.4 3.3 all-to-all-start.3
  38.2 5.0 %all-to-all-start.9 = ((bf16[2,2,64,1536]{3,2,0,1:T(8,128)(2,1)}), bf16[2,2,64,1536]{3,2,0,1:T(8,128)(2,1)S(1)}, u32[]{:S(2)}, u32[]{:S(2)}) async-start(bf16[2,2,64,1536]{3,2,0,1:T(8,128)(2,1)} %copy.129), calls=%async_computation.9 | async-start | bytes 1572864 | tf_op jit(solution)/shard_map/all_to_all | solution.py:30
  44.8 4.4 %all_to_all.112 = bf16[2,2,64,1536]{3,2,0,1:T(8,128)(2,1)S(1)} all-to-all(bf16[2,2,64,1536]{3,2,0,1:T(8,128)(2,1)S(1)} %copy.118), channel_id=1, replica_groups=mesh['ctx_0'=2,'ctx_1'=4,'ctx_2'=8,'head_0'=2,'head_1'=2] {'head_1'}, dimensions={1} | all-to-all | bytes 1572864 | tf_op jit(solution)/shard_map/all_to_all | solution.py:30
  49.1 3.3 all-to-all-start.6
  53.4 3.5 all-to-all-done.6
  56.9 3.5 all-to-all-start.10
  61.4 8.9 %all-to-all-done.10 = bf16[2,2,64,1536]{3,2,1,0:T(8,128)(2,1)S(1)} async-done(((bf16[2,2,64,1536]{3,2,1,0:T(8,128)(2,1)}), bf16[2,2,64,1536]{3,2,1,0:T(8,128)(2,1)S(1)}, u32[]{:S(2)}, u32[]{:S(2)}) %all-to-all-start.10) | async-done | bytes 786464 | tf_op jit(solution)/shard_map/all_to_all | solution.py:30
  70.2 3.5 all-to-all-start.1
  73.9 8.5 %all-to-all-done.1 = bf16[2,2,64,1536]{3,2,1,0:T(8,128)(2,1)S(1)} async-done(((bf16[2,2,64,1536]{3,2,1,0:T(8,128)(2,1)}), bf16[2,2,64,1536]{3,2,1,0:T(8,128)(2,1)S(1)}, u32[]{:S(2)}, u32[]{:S(2)}) %all-to-all-start.1) | async-done | bytes 786464 | tf_op jit(solution)/shard_map/all_to_all | solution.py:30
  83.3 5.8 %all-to-all-start.7 = ((bf16[8,2,64,256]{3,2,1,0:T(8,128)(2,1)}), bf16[8,2,64,256]{3,2,1,0:T(8,128)(2,1)S(1)}, u32[]{:S(2)}, u32[]{:S(2)}) async-start(bf16[8,2,64,256]{3,2,1,0:T(8,128)(2,1)} %stack.10), calls=%async_computation.7 | async-start | bytes 1048576 | tf_op jit(solution)/shard_map/all_to_all | solution.py:51
  95.6 6.7 %all-to-all-done.7 = bf16[8,2,64,256]{3,2,1,0:T(8,128)(2,1)S(1)} async-done(((bf16[8,2,64,256]{3,2,1,0:T(8,128)(2,1)}), bf16[8,2,64,256]{3,2,1,0:T(8,128)(2,1)S(1)}, u32[]{:S(2)}, u32[]{:S(2)}) %all-to-all-start.7) | async-done | bytes 524320 | tf_op jit(solution)/shard_map/all_to_all | solution.py:51
  103.8 4.5 %all-to-all-start.8 = ((bf16[4,16,64,256]{3,2,1,0:T(8,128)(2,1)}), bf16[4,16,64,256]{3,2,1,0:T(8,128)(2,1)}, u32[]{:S(2)}, u32[]{:S(2)}) async-start(bf16[4,16,64,256]{3,2,1,0:T(8,128)(2,1)} %stack.11), calls=%async_computation.8 | async-start | bytes 4194304 | tf_op jit(solution)/shard_map/all_to_all | solution.py:51
  137.6 3.8 collective-permute-start.2
  144.2 4.0 %collective-permute-start.3 = (bf16[256,256]{1,0:T(8,128)(2,1)S(1)}, bf16[256,256]{1,0:T(8,128)(2,1)S(1)}, u32[]{:S(2)}, u32[]{:S(2)}) collective-permute-start(bf16[256,256]{1,0:T(8,128)(2,1)S(1)} %collective-permute-done.2), channel_id=1, source_target_pairs={{0,4},{4,8},{8,12},{12,16},{16,20},{20,24},{24,28},{28,32},{32,36}... | collective-permute-start | bytes 393224 | tf_op jit(solution)/shard_map/ppermute | solution.py:43
  167.2 68.4 %while.15 = (s32[]{:T(128)}, f32[1792,128]{1,0:T(8,128)S(1)}, f32[1792,128]{1,0:T(8,128)}, f32[6,2,256,128]{3,2,1,0:T(8,128)}, pred[256,1792]{1,0:T(8,128)(4,1)S...) while((s32[]{:T(128)}, f32[1792,128]{1,0:T(8,128)S(1)}, ...), condition=%wide.region_9.10_spmd.clone, body=%wide.region_5.9_spmd.clone.sunk | while | flops 1188461568 | bytes 80503144 | solution.py:215
  186.5 3.3 fusion.70
  197.9 3.3 fusion.70
  209.4 3.3 fusion.70
  220.9 3.3 fusion.70
  232.3 3.3 fusion.70
  239.8 63.8 %reduce-scatter.4.cloned.1.call-done = f32[16,64,256]{2,1,0:T(8,128)} async-done(((f32[64,64,256]{2,1,0:T(8,128)}), f32[16,64,256]{2,1,0:T(8,128)}) %reduce-scatter.4.cloned.1.call-update) | async-done | bytes 1048592 | tf_op jit(solution)/shard_map/reduce_scatter | solution.py:68
  305.0 7.8 %collective-permute-done.4 = f32[256,256]{1,0:T(8,128)S(1)} collective-permute-done((f32[256,256]{1,0:T(8,128)S(1)}, f32[256,256]{1,0:T(8,128)S(1)}, u32[]{:S(2)}, u32[]{:S(2)}) %collective-permute-start.4) | collective-permute-done | bytes 262176 | tf_op jit(solution)/shard_map/ppermute | solution.py:43
  314.2 8.4 %collective-permute-done.5 = f32[256,256]{1,0:T(8,128)S(1)} collective-permute-done((f32[256,256]{1,0:T(8,128)S(1)}, f32[256,256]{1,0:T(8,128)S(1)}, u32[]{:S(2)}, u32[]{:S(2)}) %collective-permute-start.5) | collective-permute-done | bytes 262176 | tf_op jit(solution)/shard_map/ppermute | solution.py:43
  327.7 7.4 %all-to-all-start.11 = ((f32[4,64,1536]{2,1,0:T(8,128)}), f32[4,64,1536]{2,1,0:T(8,128)S(1)}, u32[]{:S(2)}, u32[]{:S(2)}) async-start(f32[4,64,1536]{2,1,0:T(8,128)} %all_to_all.86), calls=%async_computation.11 | async-start | bytes 3145728 | tf_op jit(solution)/shard_map/all_to_all | solution.py:247
  337.4 4.7 %reduce-scatter.6.cloned.1.call-done = f32[2,64,256]{2,1,0:T(8,128)} async-done(((f32[16,64,256]{2,1,0:T(8,128)}), f32[2,64,256]{2,1,0:T(8,128)}) %reduce-scatter.6.cloned.1.call-update) | async-done | bytes 131088 | tf_op jit(solution)/shard_map/reduce_scatter | solution.py:68
  342.1 4.2 %collective-permute-done.7 = f32[256,256]{1,0:T(8,128)S(1)} collective-permute-done((f32[256,256]{1,0:T(8,128)S(1)}, f32[256,256]{1,0:T(8,128)S(1)}, u32[]{:S(2)}, u32[]{:S(2)}) %collective-permute-start.7) | collective-permute-done | bytes 262176 | tf_op jit(solution)/shard_map/ppermute | solution.py:43
  347.2 24.5 %reduce-scatter.8.cloned.1.call-done = f32[1,64,256]{2,1,0:T(8,128)} async-done(((f32[2,64,256]{2,1,0:T(8,128)}), f32[1,64,256]{2,1,0:T(8,128)}) %reduce-scatter.8.cloned.1.call-update) | async-done | bytes 65552 | tf_op jit(solution)/shard_map/reduce_scatter | solution.py:68
  373.8 3.8 all-to-all-start.13
  381.2 4.3 %all-to-all-start.12 = ((f32[4,64,128]{2,1,0:T(8,128)}), f32[4,64,128]{2,1,0:T(8,128)S(1)}, u32[]{:S(2)}, u32[]{:S(2)}) async-start(f32[4,64,128]{2,1,0:T(8,128)} %bitcast.37), calls=%async_computation.15 | async-start | bytes 262144 | tf_op jit(solution)/shard_map/all_to_all | solution.py:248
  (265 shorter events, 127.3 us)
Async XLA Ops:
  7.2 29.6 %copy-start.10 = (bf16[64,6144]{1,0:T(8,128)(2,1)S(1)}, bf16[64,6144]{1,0:T(8,128)(2,1)}, u32[]{:S(2)}) copy-start(bf16[64,6144]{1,0:T(8,128)(2,1)} %param.9) | copy-start | bytes 2359300
  8.7 8.0 %all-to-all-start.4 = ((bf16[2,2,64,128]{3,2,0,1:T(8,128)(2,1)}), bf16[2,2,64,128]{3,2,0,1:T(8,128)(2,1)S(1)}, u32[]{:S(2)}, u32[]{:S(2)}) async-start(bf16[2,2,64,128]{3,2,0,1:T(8,128)(2,1)} %copy.125), calls=%async_computation.4 | async-start | bytes 131072 | tf_op jit(solution)/shard_map/all_to_all | solution.py:30
  16.8 4.4 %all-to-all-start.2 = ((bf16[2,2,64,128]{3,2,0,1:T(8,128)(2,1)}), bf16[2,2,64,128]{3,2,0,1:T(8,128)(2,1)S(1)}, u32[]{:S(2)}, u32[]{:S(2)}) async-start(bf16[2,2,64,128]{3,2,0,1:T(8,128)(2,1)} %copy.122), calls=%async_computation.2 | async-start | bytes 131072 | tf_op jit(solution)/shard_map/all_to_all | solution.py:30
  21.2 6.3 %all-to-all-start.5 = ((bf16[2,2,64,128]{3,2,1,0:T(8,128)(2,1)}), bf16[2,2,64,128]{3,2,1,0:T(8,128)(2,1)S(1)}, u32[]{:S(2)}, u32[]{:S(2)}) async-start(bf16[2,2,64,128]{3,2,1,0:T(8,128)(2,1)} %copy.126), calls=%async_computation.5 | async-start | bytes 131072 | tf_op jit(solution)/shard_map/all_to_all | solution.py:30
  27.4 10.7 %all-to-all-start.3 = ((bf16[2,2,64,128]{3,2,1,0:T(8,128)(2,1)}), bf16[2,2,64,128]{3,2,1,0:T(8,128)(2,1)S(1)}, u32[]{:S(2)}, u32[]{:S(2)}) async-start(bf16[2,2,64,128]{3,2,1,0:T(8,128)(2,1)} %copy.123), calls=%async_computation.3 | async-start | bytes 131072 | tf_op jit(solution)/shard_map/all_to_all | solution.py:30
  38.2 6.6 %all-to-all-start.9 = ((bf16[2,2,64,1536]{3,2,0,1:T(8,128)(2,1)}), bf16[2,2,64,1536]{3,2,0,1:T(8,128)(2,1)S(1)}, u32[]{:S(2)}, u32[]{:S(2)}) async-start(bf16[2,2,64,1536]{3,2,0,1:T(8,128)(2,1)} %copy.129), calls=%async_computation.9 | async-start | bytes 1572864 | tf_op jit(solution)/shard_map/all_to_all | solution.py:30
  43.9 29.9 %copy-start.12 = (s32[33]{0:T(128)S(1)}, s32[33]{0:T(128)}, u32[]{:S(2)}) copy-start(s32[33]{0:T(128)} %param.13) | copy-start | bytes 400
  49.1 7.8 %all-to-all-start.6 = ((bf16[2,1,64,256]{3,2,1,0:T(8,128)(2,1)}), bf16[2,1,64,256]{3,2,1,0:T(8,128)(2,1)S(1)}, u32[]{:S(2)}, u32[]{:S(2)}) async-start(bf16[2,1,64,256]{3,2,1,0:T(8,128)(2,1)} %pad_maximum_fusion.1), calls=%async_computation.6 | async-start | bytes 131072 | tf_op jit(solution)/shard_map/all_to_all | solution.py:51
  52.4 42.4 %copy-start.11 = (s32[33,4]{0,1:T(4,128)S(1)}, s32[33,4]{0,1:T(4,128)}, u32[]{:S(2)}) copy-start(s32[33,4]{0,1:T(4,128)} %param.14) | copy-start | bytes 1588
  56.9 13.3 %all-to-all-start.10 = ((bf16[2,2,64,1536]{3,2,1,0:T(8,128)(2,1)}), bf16[2,2,64,1536]{3,2,1,0:T(8,128)(2,1)S(1)}, u32[]{:S(2)}, u32[]{:S(2)}) async-start(bf16[2,2,64,1536]{3,2,1,0:T(8,128)(2,1)} %copy.130), calls=%async_computation.10 | async-start | bytes 1572864 | tf_op jit(solution)/shard_map/all_to_all | solution.py:30
  70.2 12.2 %all-to-all-start.1 = ((bf16[2,2,64,1536]{3,2,1,0:T(8,128)(2,1)}), bf16[2,2,64,1536]{3,2,1,0:T(8,128)(2,1)S(1)}, u32[]{:S(2)}, u32[]{:S(2)}) async-start(bf16[2,2,64,1536]{3,2,1,0:T(8,128)(2,1)} %copy.119), calls=%async_computation.1 | async-start | bytes 1572864 | tf_op jit(solution)/shard_map/all_to_all | solution.py:30
  82.4 21.4 %copy-start.9 = (bf16[2,2,64,1536]{3,2,1,0:T(8,128)(2,1)}, bf16[2,2,64,1536]{3,2,1,0:T(8,128)(2,1)S(1)}, u32[]{:S(2)}) copy-start(bf16[2,2,64,1536]{3,2,1,0:T(8,128)(2,1)S(1)} %all-to-all-done.1) | copy-start | bytes 2359300
  83.3 19.0 %all-to-all-start.7 = ((bf16[8,2,64,256]{3,2,1,0:T(8,128)(2,1)}), bf16[8,2,64,256]{3,2,1,0:T(8,128)(2,1)S(1)}, u32[]{:S(2)}, u32[]{:S(2)}) async-start(bf16[8,2,64,256]{3,2,1,0:T(8,128)(2,1)} %stack.10), calls=%async_computation.7 | async-start | bytes 1048576 | tf_op jit(solution)/shard_map/all_to_all | solution.py:51
  95.1 14.8 %copy-start.13 = (s32[33]{0:T(128)S(1)}, s32[33]{0:T(128)}, u32[]{:S(2)}) copy-start(s32[33]{0:T(128)} %param.15) | copy-start | bytes 400
  103.8 55.5 %all-to-all-start.8 = ((bf16[4,16,64,256]{3,2,1,0:T(8,128)(2,1)}), bf16[4,16,64,256]{3,2,1,0:T(8,128)(2,1)}, u32[]{:S(2)}, u32[]{:S(2)}) async-start(bf16[4,16,64,256]{3,2,1,0:T(8,128)(2,1)} %stack.11), calls=%async_computation.8 | async-start | bytes 4194304 | tf_op jit(solution)/shard_map/all_to_all | solution.py:51
  108.3 195.4 %reduce-scatter.4.cloned.1.call-start = ((), (), s32[]{:S(2)}) async-start(), calls=%async_computation.17 | async-start | bytes 5242880 | tf_op jit(solution)/shard_map/reduce_scatter | solution.py:68
  108.4 24.2 %collective-permute-start = (bf16[256,256]{1,0:T(8,128)(2,1)S(1)}, bf16[256,256]{1,0:T(8,128)(2,1)S(1)}, u32[]{:S(2)}, u32[]{:S(2)}) collective-permute-start(bf16[256,256]{1,0:T(8,128)(2,1)S(1)} %pad_maximum_fusion), channel_id=1, source_target_pairs={{0,4},{4,8},{8,12},{12,16},{16,20},{20,24},{24,28},{28,32},{32,36}... | collective-permute-start | bytes 393224 | tf_op jit(solution)/shard_map/ppermute | solution.py:43
  132.6 5.0 %collective-permute-start.1 = (bf16[256,256]{1,0:T(8,128)(2,1)S(1)}, bf16[256,256]{1,0:T(8,128)(2,1)S(1)}, u32[]{:S(2)}, u32[]{:S(2)}) collective-permute-start(bf16[256,256]{1,0:T(8,128)(2,1)S(1)} %collective-permute-done), channel_id=1, source_target_pairs={{0,4},{4,8},{8,12},{12,16},{16,20},{20,24},{24,28},{28,32},{32,36}... | collective-permute-start | bytes 393224 | tf_op jit(solution)/shard_map/ppermute | solution.py:43
  137.6 6.6 %collective-permute-start.2 = (bf16[256,256]{1,0:T(8,128)(2,1)S(1)}, bf16[256,256]{1,0:T(8,128)(2,1)S(1)}, u32[]{:S(2)}, u32[]{:S(2)}) collective-permute-start(bf16[256,256]{1,0:T(8,128)(2,1)S(1)} %collective-permute-done.1), channel_id=1, source_target_pairs={{0,4},{4,8},{8,12},{12,16},{16,20},{20,24},{24,28},{28,32},{32,36}... | collective-permute-start | bytes 393224 | tf_op jit(solution)/shard_map/ppermute | solution.py:43
  144.2 11.7 %collective-permute-start.3 = (bf16[256,256]{1,0:T(8,128)(2,1)S(1)}, bf16[256,256]{1,0:T(8,128)(2,1)S(1)}, u32[]{:S(2)}, u32[]{:S(2)}) collective-permute-start(bf16[256,256]{1,0:T(8,128)(2,1)S(1)} %collective-permute-done.2), channel_id=1, source_target_pairs={{0,4},{4,8},{8,12},{12,16},{16,20},{20,24},{24,28},{28,32},{32,36}... | collective-permute-start | bytes 393224 | tf_op jit(solution)/shard_map/ppermute | solution.py:43
  178.3 3.6 copy-start.6
  189.8 3.6 copy-start.6
  236.9 85.7 %copy-start.8 = (f32[1792,256]{1,0:T(8,128)}, f32[1792,256]{1,0:T(8,128)S(1)}, u32[]{:S(2)}) copy-start(f32[1792,256]{1,0:T(8,128)S(1)} %constant_dynamic-update-slice_fusion.13) | copy-start | bytes 5505028
  239.8 102.3 %reduce-scatter.6.cloned.1.call-start = ((), (), s32[]{:S(2)}) async-start(), calls=%async_computation.18 | async-start | bytes 1179648 | tf_op jit(solution)/shard_map/reduce_scatter | solution.py:68
  303.7 9.1 %collective-permute-start.4 = (f32[256,256]{1,0:T(8,128)S(1)}, f32[256,256]{1,0:T(8,128)S(1)}, u32[]{:S(2)}, u32[]{:S(2)}) collective-permute-start(f32[256,256]{1,0:T(8,128)S(1)} %slice.128), channel_id=1, source_target_pairs={{4,0},{8,4},{12,8},{16,12},{20,16},{24,20},{28,24},{32,28},{36,32}... | collective-permute-start | bytes 786440 | tf_op jit(solution)/shard_map/ppermute | solution.py:43
  312.9 9.7 %collective-permute-start.5 = (f32[256,256]{1,0:T(8,128)S(1)}, f32[256,256]{1,0:T(8,128)S(1)}, u32[]{:S(2)}, u32[]{:S(2)}) collective-permute-start(f32[256,256]{1,0:T(8,128)S(1)} %slice_add_fusion.2), channel_id=1, source_target_pairs={{4,0},{8,4},{12,8},{16,12},{20,16},{24,20},{28,24},{32,28},{36,32}... | collective-permute-start | bytes 786440 | tf_op jit(solution)/shard_map/ppermute | solution.py:43
  322.6 12.5 %collective-permute-start.6 = (f32[256,256]{1,0:T(8,128)S(1)}, f32[256,256]{1,0:T(8,128)S(1)}, u32[]{:S(2)}, u32[]{:S(2)}) collective-permute-start(f32[256,256]{1,0:T(8,128)S(1)} %slice_add_fusion.1), channel_id=1, source_target_pairs={{4,0},{8,4},{12,8},{16,12},{20,16},{24,20},{28,24},{32,28},{36,32}... | collective-permute-start | bytes 786440 | tf_op jit(solution)/shard_map/ppermute | solution.py:43
  327.7 46.1 %all-to-all-start.11 = ((f32[4,64,1536]{2,1,0:T(8,128)}), f32[4,64,1536]{2,1,0:T(8,128)S(1)}, u32[]{:S(2)}, u32[]{:S(2)}) async-start(f32[4,64,1536]{2,1,0:T(8,128)} %all_to_all.86), calls=%async_computation.11 | async-start | bytes 3145728 | tf_op jit(solution)/shard_map/all_to_all | solution.py:247
  335.1 36.6 %reduce-scatter.8.cloned.1.call-start = ((), (), s32[]{:S(2)}) async-start(), calls=%async_computation.19 | async-start | bytes 196608 | tf_op jit(solution)/shard_map/reduce_scatter | solution.py:68
  336.1 10.2 %collective-permute-start.7 = (f32[256,256]{1,0:T(8,128)S(1)}, f32[256,256]{1,0:T(8,128)S(1)}, u32[]{:S(2)}, u32[]{:S(2)}) collective-permute-start(f32[256,256]{1,0:T(8,128)S(1)} %slice_add_fusion), channel_id=1, source_target_pairs={{4,0},{8,4},{12,8},{16,12},{20,16},{24,20},{28,24},{32,28},{36,32}... | collective-permute-start | bytes 786440 | tf_op jit(solution)/shard_map/ppermute | solution.py:43
  373.8 7.4 %all-to-all-start.13 = ((f32[4,64,128]{2,1,0:T(8,128)}), f32[4,64,128]{2,1,0:T(8,128)S(1)}, u32[]{:S(2)}, u32[]{:S(2)}) async-start(f32[4,64,128]{2,1,0:T(8,128)} %bitcast.39), calls=%async_computation.16 | async-start | bytes 262144 | tf_op jit(solution)/shard_map/all_to_all | solution.py:249
  381.2 7.9 %all-to-all-start.12 = ((f32[4,64,128]{2,1,0:T(8,128)}), f32[4,64,128]{2,1,0:T(8,128)S(1)}, u32[]{:S(2)}, u32[]{:S(2)}) async-start(f32[4,64,128]{2,1,0:T(8,128)} %bitcast.37), calls=%async_computation.15 | async-start | bytes 262144 | tf_op jit(solution)/shard_map/all_to_all | solution.py:248
  (46 other events, 129.0 us)
Sparse Core Ops, SparseCore 0:
  239.9 63.7 reduce-scatter.3
  306.3 35.6 reduce-scatter.5
  344.7 26.9 reduce-scatter.7
